TPU v7x, 32 devices: a whole 2x2x4 slice. The times are simulated.
32 devices in a mesh: fsdp: 16 (over z, y, x), tensor: 2 (over core).
Axes of the slice: x: 2, y: 2, z: 4, core: 2. Of those that a mesh axis runs over, the one named last changes fastest.
Arguments:
- tokens: bfloat16 [16384, 1024], P('fsdp'), may hold values from -6 to 6
- lengths: int32 [16, 8], P('fsdp'), may hold values from 1 to 512, 1024 in all within a row
- w_query: bfloat16 [1024, 1024], P('fsdp', 'tensor'), may hold values from -0.1875 to 0.1875
- key_weight: bfloat16 [1024, 512], P('fsdp', 'tensor'), may hold values from -0.1875 to 0.1875
- value_weight: bfloat16 [1024, 512], P('fsdp', 'tensor'), may hold values from -0.1875 to 0.1875
- w_output: bfloat16 [1024, 1024], P('tensor', 'fsdp'), may hold values from -1.5 to 1.5
- w_gate: bfloat16 [1024, 4608], P('fsdp', 'tensor'), may hold values from -0.1875 to 0.1875
- w_up: bfloat16 [1024, 4608], P('fsdp', 'tensor'), may hold values from -0.1875 to 0.1875
- w_down: bfloat16 [4608, 1024], P('tensor', 'fsdp'), may hold values from -0.09375 to 0.09375
- gain_attn: bfloat16 [1024], P('fsdp'), may hold values from 0.099609375 to 1.8984375
- gain_ffn: bfloat16 [1024], P('fsdp'), may hold values from 0.099609375 to 1.8984375
- gain_query: bfloat16 [64], replicated, may hold values from 0.099609375 to 1.8984375
- key_norm_gain: bfloat16 [64], replicated, may hold values from 0.099609375 to 1.8984375
- cotangent: bfloat16 [16384, 1024], P('fsdp'), may hold values from -6 to 6
Outputs:
- layer_out: bfloat16 [16384, 1024], P('fsdp')
- token_grad: bfloat16 [16384, 1024], P('fsdp')
- grad_query: float32 [1024, 1024], P('fsdp', 'tensor')
- grad_key: float32 [1024, 512], P('fsdp', 'tensor')
- grad_value: float32 [1024, 512], P('fsdp', 'tensor')
- grad_output: float32 [1024, 1024], P('tensor', 'fsdp')
- grad_gate: float32 [1024, 4608], P('fsdp', 'tensor')
- grad_up: float32 [1024, 4608], P('fsdp', 'tensor')
- grad_down: float32 [4608, 1024], P('tensor', 'fsdp')
- grad_gain_attn: float32 [1024], P('fsdp')
- grad_gain_ffn: float32 [1024], P('fsdp')
- grad_gain_query: float32 [64], replicated
- grad_gain_key: float32 [64], replicated
Inputs may be any that keep to these rules, and one draw needn't show every extreme that they name: Each lengths row sums to 1024 and holds one length of exactly 512.
All inputs are finite; a program needn't handle non-finite values.
Results may differ from a plain program's by a relative error of at most 0.014.
Values may be sent and summed in bfloat16 or wider, within the bound.
A program may use at most 192 MiB of HBM per device.

v0:
```python
import jax
import jax.numpy as jnp
from jax import lax
from jax.sharding import PartitionSpec as P

HEAD_SIZE = 64
QUERY_GROUP = 2
QUERY_BLOCK_ROWS = 512


EPS = 1e-05
THETA = 1000000.0


def root_mean_scale(value, gain):
    return value * lax.rsqrt(jnp.mean(value * value, axis=-1, keepdims=True) + EPS) * gain


def apply_rotary(value, cosine_table, sine_table):
    half = value.shape[-1] // 2
    first = value[..., :half]
    second = value[..., half:]
    return jnp.concatenate(
        [first * cosine_table - second * sine_table, second * cosine_table + first * sine_table],
        axis=-1,
    )


def prepare(raw, gain, cosine_table, sine_table):
    count = raw.shape[0]
    heads = raw.reshape(count, -1, gain.shape[0])
    return apply_rotary(root_mean_scale(heads, gain), cosine_table, sine_table).reshape(count, -1)


def swish_product(gate, upward):
    return gate * jax.nn.sigmoid(gate) * upward


def matrix_product(left, right):
    return jnp.dot(left, right, preferred_element_type=jnp.float32)


def matmul_t(left, right):
    return lax.dot_general(
        left, right, (((1,), (1,)), ((), ())), preferred_element_type=jnp.float32
    )


def inner_rows(left, right):
    return lax.dot_general(
        left, right, (((0,), (0,)), ((), ())), preferred_element_type=jnp.float32
    )


def local(
    tokens,
    lengths,
    w_query,
    key_weight,
    value_weight,
    w_output,
    w_gate,
    w_up,
    w_down,
    gain_attn,
    gain_ffn,
    gain_query,
    key_norm_gain,
    cotangent,
):
    rows = tokens.shape[0]
    scale = HEAD_SIZE ** (-0.5)
    blocks = rows // QUERY_BLOCK_ROWS
    lens = lengths[0]
    ends = jnp.cumsum(lens)
    row_ids = jnp.arange(rows, dtype=jnp.int32)
    passed = row_ids[:, None] >= ends[None, :]
    segment = jnp.sum(passed.astype(jnp.int32), axis=1)
    begin = jnp.sum(jnp.where(passed, lens[None, :], 0), axis=1)
    position = (row_ids - begin).astype(jnp.float32)
    freq = THETA ** (-jnp.arange(HEAD_SIZE // 2, dtype=jnp.float32) * 2.0 / HEAD_SIZE)
    angle = position[:, None] * freq[None, :]
    cosine_table = jnp.cos(angle)[:, None, :]
    sine_table = jnp.sin(angle)[:, None, :]
    attn_set = (
        lax.all_gather(w_query, "fsdp", axis=0, tiled=True),
        lax.all_gather(key_weight, "fsdp", axis=0, tiled=True),
        lax.all_gather(value_weight, "fsdp", axis=0, tiled=True),
        lax.all_gather(w_output, "fsdp", axis=1, tiled=True),
        lax.all_gather(gain_attn, "fsdp", axis=0, tiled=True),
    )
    ffn_set = (
        lax.all_gather(w_gate, "fsdp", axis=0, tiled=True),
        lax.all_gather(w_up, "fsdp", axis=0, tiled=True),
        lax.all_gather(w_down, "fsdp", axis=1, tiled=True),
        lax.all_gather(gain_ffn, "fsdp", axis=0, tiled=True),
    )
    query_all, key_all, value_all, output_all, first_gain = attn_set
    gate_all, up_all, down_all, second_gain = ffn_set
    first_gain = first_gain.astype(jnp.float32)
    second_gain = second_gain.astype(jnp.float32)
    query_gain = gain_query.astype(jnp.float32)
    key_gain = key_norm_gain.astype(jnp.float32)
    x_float = tokens.astype(jnp.float32)
    first_hidden = root_mean_scale(x_float, first_gain).astype(jnp.bfloat16)
    q_raw = matrix_product(first_hidden, query_all)
    key_unnormed = matrix_product(first_hidden, key_all)
    value_rounded_copy = matrix_product(first_hidden, value_all).astype(jnp.bfloat16)
    query_rounded_copy = prepare(q_raw, query_gain, cosine_table, sine_table).astype(jnp.bfloat16)
    key_rounded_copy = prepare(key_unnormed, key_gain, cosine_table, sine_table).astype(
        jnp.bfloat16
    )
    kv_heads = key_rounded_copy.shape[1] // HEAD_SIZE
    width = query_rounded_copy.shape[1]
    key_rows = key_rounded_copy.reshape(rows, kv_heads, HEAD_SIZE)
    value_rows = value_rounded_copy.reshape(rows, kv_heads, HEAD_SIZE)

    def block_scores(start_offset):
        query_block_slice = lax.dynamic_slice_in_dim(
            query_rounded_copy, start_offset, QUERY_BLOCK_ROWS, 0
        ).reshape(QUERY_BLOCK_ROWS, kv_heads, QUERY_GROUP, HEAD_SIZE)
        scores = (
            jnp.einsum(
                "bkgd,skd->kgbs", query_block_slice, key_rows, preferred_element_type=jnp.float32
            )
            * scale
        )
        block_rows = start_offset + jnp.arange(QUERY_BLOCK_ROWS, dtype=jnp.int32)
        seg_rows = lax.dynamic_slice_in_dim(segment, start_offset, QUERY_BLOCK_ROWS, 0)
        allowed = (seg_rows[:, None] == segment[None, :]) & (
            row_ids[None, :] <= block_rows[:, None]
        )
        return (query_block_slice, jnp.where(allowed, scores, -1e30))

    def forward_block(start_offset):
        query_block_slice, scores = block_scores(start_offset)
        top = jnp.max(scores, axis=-1, keepdims=True)
        weights = jnp.exp(scores - top)
        total = jnp.sum(weights, axis=-1, keepdims=True)
        prob = (weights / total).astype(jnp.bfloat16)
        out = jnp.einsum(
            "kgbs,skd->bkgd", prob, value_rows, preferred_element_type=jnp.float32
        ).reshape(QUERY_BLOCK_ROWS, width)
        return (out, top + jnp.log(total))

    starts = jnp.arange(blocks, dtype=jnp.int32) * QUERY_BLOCK_ROWS
    attended_blocks, log_totals = lax.map(forward_block, starts)
    attended = attended_blocks.reshape(rows, width).astype(jnp.bfloat16)
    branch = lax.psum(matrix_product(attended, output_all), "tensor")
    resid = x_float + branch
    h_second = root_mean_scale(resid, second_gain).astype(jnp.bfloat16)
    gate = matrix_product(h_second, gate_all)
    upward = matrix_product(h_second, up_all)
    hidden = swish_product(gate, upward).astype(jnp.bfloat16)
    ffn_out = lax.psum(matrix_product(hidden, down_all).astype(jnp.bfloat16), "tensor").astype(
        jnp.float32
    )
    layer_out = (resid + ffn_out).astype(jnp.bfloat16)
    dy_float = cotangent.astype(jnp.float32)
    grad_down = inner_rows(hidden, cotangent)
    d_hidden = matmul_t(cotangent, down_all)
    unused_value, pull_swish = jax.vjp(swish_product, gate, upward)
    d_gate, d_up = pull_swish(d_hidden)
    d_gate = d_gate.astype(jnp.bfloat16)
    d_up = d_up.astype(jnp.bfloat16)
    grad_gate = inner_rows(h_second, d_gate)
    grad_up = inner_rows(h_second, d_up)
    d_second = lax.psum(matmul_t(d_gate, gate_all) + matmul_t(d_up, up_all), "tensor")
    unused_norm, pull_second = jax.vjp(root_mean_scale, resid, second_gain)
    d_resid_norm, grad_second_gain = pull_second(d_second)
    d_resid = dy_float + d_resid_norm
    d_branch = d_resid.astype(jnp.bfloat16)
    grad_output = inner_rows(attended, d_branch)
    d_attended = matmul_t(d_branch, output_all).astype(jnp.bfloat16)

    def backward_block(carry, index):
        key_acc, value_acc = carry
        start_offset = index * QUERY_BLOCK_ROWS
        query_block_slice, scores = block_scores(start_offset)
        prob = jnp.exp(scores - log_totals[index])
        d_block = lax.dynamic_slice_in_dim(d_attended, start_offset, QUERY_BLOCK_ROWS, 0).reshape(
            QUERY_BLOCK_ROWS, kv_heads, QUERY_GROUP, HEAD_SIZE
        )
        d_prob = jnp.einsum(
            "bkgd,skd->kgbs", d_block, value_rows, preferred_element_type=jnp.float32
        )
        delta = jnp.sum(d_prob * prob, axis=-1, keepdims=True)
        d_scores = (prob * (d_prob - delta)).astype(jnp.bfloat16)
        d_query_block = (
            jnp.einsum("kgbs,skd->bkgd", d_scores, key_rows, preferred_element_type=jnp.float32)
            * scale
        )
        key_acc = (
            key_acc
            + jnp.einsum(
                "kgbs,bkgd->skd", d_scores, query_block_slice, preferred_element_type=jnp.float32
            )
            * scale
        )
        value_acc = value_acc + jnp.einsum(
            "kgbs,bkgd->skd", prob.astype(jnp.bfloat16), d_block, preferred_element_type=jnp.float32
        )
        return ((key_acc, value_acc), d_query_block.reshape(QUERY_BLOCK_ROWS, width))

    empty = jnp.zeros((rows, kv_heads, HEAD_SIZE), jnp.float32)
    (d_key_round, d_value), d_query_blocks = lax.scan(
        backward_block, (empty, empty), jnp.arange(blocks, dtype=jnp.int32)
    )
    d_query_round = d_query_blocks.reshape(rows, width)
    unused_query, pull_query = jax.vjp(
        lambda raw, gain: prepare(raw, gain, cosine_table, sine_table), q_raw, query_gain
    )
    d_q_raw, grad_query_gain = pull_query(d_query_round)
    unused_key, pull_key = jax.vjp(
        lambda raw, gain: prepare(raw, gain, cosine_table, sine_table), key_unnormed, key_gain
    )
    d_k_raw, grad_key_gain = pull_key(d_key_round.reshape(rows, kv_heads * HEAD_SIZE))
    d_q_raw = d_q_raw.astype(jnp.bfloat16)
    d_k_raw = d_k_raw.astype(jnp.bfloat16)
    d_value = d_value.reshape(rows, kv_heads * HEAD_SIZE).astype(jnp.bfloat16)
    grad_query = inner_rows(first_hidden, d_q_raw)
    grad_key = inner_rows(first_hidden, d_k_raw)
    grad_value = inner_rows(first_hidden, d_value)
    grad_query_gain, grad_key_gain = lax.psum((grad_query_gain, grad_key_gain), ("fsdp", "tensor"))
    d_first_part = (
        matmul_t(d_q_raw, query_all) + matmul_t(d_k_raw, key_all) + matmul_t(d_value, value_all)
    )
    d_first = lax.psum(d_first_part.astype(jnp.bfloat16), "tensor").astype(jnp.float32)
    unused_first_norm, pull_first = jax.vjp(root_mean_scale, x_float, first_gain)
    d_x_norm, grad_first_gain = pull_first(d_first)
    token_grad = (d_resid + d_x_norm).astype(jnp.bfloat16)
    summed = (
        lax.psum_scatter(grad_query, "fsdp", scatter_dimension=0, tiled=True),
        lax.psum_scatter(grad_key, "fsdp", scatter_dimension=0, tiled=True),
        lax.psum_scatter(grad_value, "fsdp", scatter_dimension=0, tiled=True),
        lax.psum_scatter(grad_output, "fsdp", scatter_dimension=1, tiled=True),
        lax.psum_scatter(grad_gate, "fsdp", scatter_dimension=0, tiled=True),
        lax.psum_scatter(grad_up, "fsdp", scatter_dimension=0, tiled=True),
        lax.psum_scatter(grad_down, "fsdp", scatter_dimension=1, tiled=True),
        lax.psum_scatter(grad_first_gain, "fsdp", scatter_dimension=0, tiled=True),
        lax.psum_scatter(grad_second_gain, "fsdp", scatter_dimension=0, tiled=True),
    )
    (
        shard_query,
        shard_key,
        shard_value,
        shard_output,
        shard_gate,
        shard_up,
        shard_down,
        shard_first,
        shard_second,
    ) = summed
    return (
        layer_out,
        token_grad,
        shard_query,
        shard_key,
        shard_value,
        shard_output,
        shard_gate,
        shard_up,
        shard_down,
        shard_first,
        shard_second,
        grad_query_gain,
        grad_key_gain,
    )


def solution(mesh):
    return jax.shard_map(
        local,
        mesh=mesh,
        in_specs=(
            P("fsdp", None),
            P("fsdp", None),
            P("fsdp", "tensor"),
            P("fsdp", "tensor"),
            P("fsdp", "tensor"),
            P("tensor", "fsdp"),
            P("fsdp", "tensor"),
            P("fsdp", "tensor"),
            P("tensor", "fsdp"),
            P("fsdp"),
            P("fsdp"),
            P(),
            P(),
            P("fsdp", None),
        ),
        out_specs=(
            P("fsdp", None),
            P("fsdp", None),
            P("fsdp", "tensor"),
            P("fsdp", "tensor"),
            P("fsdp", "tensor"),
            P("tensor", "fsdp"),
            P("fsdp", "tensor"),
            P("fsdp", "tensor"),
            P("tensor", "fsdp"),
            P("fsdp"),
            P("fsdp"),
            P(),
            P(),
        ),
        check_vma=False,
    )
```

profile of v0, /device:TPU:0, one launch (start us, length us, event | category | flops | bytes accessed | tf_op | source)
XLA Modules:
  0.0 1608.4 jit_solution(3456454114907143207)
XLA Ops:
  13.9 44.3 %all-reduce.10 = (bf16[1024]{0:T(1024)(128)(2,1)S(1)}, bf16[1024]{0:T(1024)(128)(2,1)}) all-reduce(bf16[1024]{0:T(1024)(128)(2,1)S(1)} %dynamic-update-slice, bf16[1024]{0:T(1024)(128)(2,1)S(1)} %dynamic-update-slice.1), channel_id=1, replica_groups=mesh['fsdp'=16,'tensor'=2] {'fsdp'}, use_global_device_ids=true, to_apply=%add.4 | all-reduce | flops 2048 | bytes 8192
  61.9 39.5 %all_gather.29 = bf16[1024,256]{1,0:T(8,128)(2,1)S(1)} all-gather(bf16[64,256]{1,0:T(8,128)(2,1)} %param.21), channel_id=1, replica_groups=mesh['fsdp'=16,'tensor'=2] {'fsdp'}, dimensions={0}, use_global_device_ids=true | all-gather | bytes 557056 | tf_op jit(solution)/shard_map/all_gather | solution.py:87
  104.3 40.8 %all_gather.30 = bf16[1024,256]{1,0:T(8,128)(2,1)S(1)} all-gather(bf16[64,256]{1,0:T(8,128)(2,1)S(1)} %copy-done.49), channel_id=1, replica_groups=mesh['fsdp'=16,'tensor'=2] {'fsdp'}, dimensions={0}, use_global_device_ids=true | all-gather | bytes 557056 | tf_op jit(solution)/shard_map/all_gather | solution.py:88
  152.6 39.0 %while.28 = (s32[]{:T(128)}, bf16[2,512,512]{2,1,0:T(8,128)(2,1)}, f32[2,4,2,512,1]{3,2,1,4,0:T(2,128)S(1)}, s32[2]{0:T(128)S(1)}, s32[1024]{0:T(1024)S(1)}, /*i...) while((s32[]{:T(128)}, bf16[2,512,512]{2,1,0:T(8,128)(2,1)}, ...), condition=%wide.region_9.10_spmd.clone, body=%wide.region_6.9_spmd.clone.sunk | while | flops 1125642752 | bytes 57817272 | solution.py:147
  161.8 4.3 fusion.140
  166.1 5.0 fusion.141
  181.3 4.3 fusion.140
  185.6 5.0 fusion.141
  191.7 4.8 fusion.67
  198.8 22.9 %all-reduce.16.cloned.1.call-done = f32[1024,1024]{1,0:T(8,128)} async-done(((f32[1024,1024]{1,0:T(8,128)}), f32[1024,1024]{1,0:T(8,128)}) %all-reduce.16.cloned.1.call-update) | async-done | bytes 4194320 | tf_op jit(solution)/shard_map/psum | solution.py:149
  226.9 79.5 %all-gather.10.cloned.1.call-done = bf16[1024,2304]{1,0:T(8,128)(2,1)} async-done(((bf16[64,2304]{1,0:T(8,128)(2,1)}), bf16[1024,2304]{1,0:T(8,128)(2,1)}) %all-gather.10.cloned.1.call-update) | async-done | bytes 4718608 | tf_op jit(solution)/shard_map/all_gather | solution.py:93
  306.4 9.7 fusion.68
  316.2 72.4 %all-gather.12.cloned.1.call-done = bf16[1024,2304]{1,0:T(8,128)(2,1)} async-done(((bf16[64,2304]{1,0:T(8,128)(2,1)}), bf16[1024,2304]{1,0:T(8,128)(2,1)}) %all-gather.12.cloned.1.call-update) | async-done | bytes 4718608 | tf_op jit(solution)/shard_map/all_gather | solution.py:94
  388.6 9.7 fusion.69
  398.3 72.5 %all-gather.14.cloned.1.call-done = bf16[2304,1024]{0,1:T(8,128)(2,1)} async-done(((bf16[2304,64]{0,1:T(8,128)(2,1)}), bf16[2304,1024]{0,1:T(8,128)(2,1)}) %all-gather.14.cloned.1.call-update) | async-done | bytes 4718608 | tf_op jit(solution)/shard_map/all_gather | solution.py:95
  470.7 16.4 %multiply_convert_fusion = (bf16[1024,2304]{1,0:T(8,128)(2,1)S(1)}, bf16[1024,2304]{1,0:T(8,128)(2,1)S(1)}, bf16[1024,2304]{1,0:T(8,128)(2,1)}) fusion(f32[1024,2304]{1,0:T(8,128)} %fusion.68, f32[1024,2304]{1,0:T(8,128)} %fusion.69, bf16[1024,1024]{1,0:T(8,128)(2,1)} %param.31, bf16[2304,1024]{0,1:T(8,128)(2,1)} %all-gather.14.cloned.1.call-done), kind=kOutput, calls=%fused_computation.50 | convolution fusion | flops 4869586944 | bytes 39845888 | tf_op jit(solution)/shard_map/dot_general | solution.py:44
  487.1 8.9 fusion.70
  496.0 6.7 convolution_add_fusion
  502.8 9.4 convolution_convert_fusion
  512.3 17.6 %all-reduce.18.cloned.1.call-done = f32[1024,1024]{1,0:T(8,128)} async-done(((f32[1024,1024]{1,0:T(8,128)}), f32[1024,1024]{1,0:T(8,128)}) %all-reduce.18.cloned.1.call-update) | async-done | bytes 4194320 | tf_op jit(solution)/shard_map/psum | solution.py:168
  529.9 5.2 multiply_reduce_fusion
  539.5 161.8 %while.29 = (s32[]{:T(128)}, f32[1024,4,64]{0,2,1:T(8,128)}, f32[1024,4,64]{0,2,1:T(8,128)}, f32[2,512,512]{1,0,2:T(2,128)}, s32[2]{0:T(128)S(1)}, /*index=5*/bf...) while((s32[]{:T(128)}, f32[1024,4,64]{0,2,1:T(8,128)}, ...), condition=%wide.region_17.18_spmd.clone, body=%wide.region_15.17_spmd.clone.sunk | while | flops 2725245440 | bytes 233667216 | solution.py:206
  544.3 8.1 fusion.151
  555.9 15.5 fusion.153
  572.2 9.5 fusion.154
  581.7 6.2 fusion.155
  587.8 7.7 fusion.156
  600.7 19.5 %dynamic_update_slice.21 = f32[2,512,512]{1,0,2:T(2,128)} dynamic-update-slice(f32[2,512,512]{1,0,2:T(2,128)} %get-tuple-element.487, f32[1,512,512]{1,0,2:T(1,128)S(1)} %copy.69, s32[]{:T(128)S(6)} %copy.90, s32[]{:T(128)} %constant.44.clone.1..sunk.1, s32[]{:T(128)} %constant.44.clone.1..sunk.1) | dynamic-update-slice | bytes 2097156 | tf_op jit(solution)/shard_map/while/body/jit(dynamic_update_index_in_dim)/dynamic_update_slice | solution.py:147
  625.0 8.1 fusion.151
  636.5 15.5 fusion.153
  652.8 9.5 fusion.154
  662.3 6.4 fusion.155
  668.6 7.7 fusion.156
  681.6 19.5 %dynamic_update_slice.21 = f32[2,512,512]{1,0,2:T(2,128)} dynamic-update-slice(f32[2,512,512]{1,0,2:T(2,128)} %get-tuple-element.487, f32[1,512,512]{1,0,2:T(1,128)S(1)} %copy.69, s32[]{:T(128)S(6)} %copy.90, s32[]{:T(128)} %constant.44.clone.1..sunk.1, s32[]{:T(128)} %constant.44.clone.1..sunk.1) | dynamic-update-slice | bytes 2097156 | tf_op jit(solution)/shard_map/while/body/jit(dynamic_update_index_in_dim)/dynamic_update_slice | solution.py:147
  710.6 4.2 reshape_reshape.3
  734.1 5.4 fusion.48
  739.7 10.4 fusion.73
  750.1 10.4 fusion.74
  760.6 10.2 fusion.75
  771.5 40.9 %all-reduce.8 = (f32[64]{0:T(128)}, f32[64]{0:T(128)}) all-reduce(f32[64]{0:T(128)S(1)} %get-tuple-element.234, f32[64]{0:T(128)S(1)} %get-tuple-element.236), channel_id=1, replica_groups=mesh['fsdp'=16,'tensor'=2] {'fsdp','tensor'}, use_global_device_ids=true, to_apply=%region_34.35 | all-reduce | flops 128 | bytes 1024 | tf_op jit(solution)/shard_map/psum | solution.py:224
  815.7 41.4 %all-reduce.9 = (f32[1024]{0:T(1024)S(1)}, f32[1024]{0:T(1024)S(1)}) all-reduce(f32[1024]{0:T(1024)S(1)} %get-tuple-element.232, f32[1024]{0:T(1024)S(1)} %copy-done.50), channel_id=9, replica_groups=mesh['fsdp'=16,'tensor'=2] {'fsdp'}, use_global_device_ids=true, to_apply=%region_30.31.clone | all-reduce | flops 2048 | bytes 16384
  858.3 5.1 add_convert_fusion.1
  865.8 46.2 %reduce-scatter.12.cloned.1.call-done = f32[64,256]{1,0:T(8,128)} async-done(((f32[1024,256]{1,0:T(8,128)}), f32[64,256]{1,0:T(8,128)}) %reduce-scatter.12.cloned.1.call-update) | async-done | bytes 65552 | tf_op jit(solution)/shard_map/reduce_scatter | solution.py:235
  912.0 79.7 %reduce-scatter.8.cloned.1.call-done = f32[64,512]{1,0:T(8,128)} async-done(((f32[1024,512]{1,0:T(8,128)}), f32[64,512]{1,0:T(8,128)}) %reduce-scatter.8.cloned.1.call-update) | async-done | bytes 131088 | tf_op jit(solution)/shard_map/reduce_scatter | solution.py:233
  991.7 80.5 %reduce-scatter.14.cloned.1.call-done = f32[512,64]{0,1:T(8,128)} async-done(((f32[512,1024]{0,1:T(8,128)}), f32[512,64]{0,1:T(8,128)}) %reduce-scatter.14.cloned.1.call-update) | async-done | bytes 131088 | tf_op jit(solution)/shard_map/reduce_scatter | solution.py:236
  1072.2 175.7 %reduce-scatter.16.cloned.1.call-done = f32[64,2304]{1,0:T(8,128)} async-done(((f32[1024,2304]{1,0:T(8,128)}), f32[64,2304]{1,0:T(8,128)}) %reduce-scatter.16.cloned.1.call-update) | async-done | bytes 589840 | tf_op jit(solution)/shard_map/reduce_scatter | solution.py:237
  1247.9 176.3 %reduce-scatter.18.cloned.1.call-done = f32[64,2304]{1,0:T(8,128)} async-done(((f32[1024,2304]{1,0:T(8,128)}), f32[64,2304]{1,0:T(8,128)}) %reduce-scatter.18.cloned.1.call-update) | async-done | bytes 589840 | tf_op jit(solution)/shard_map/reduce_scatter | solution.py:238
  1424.2 177.2 %reduce-scatter.20.cloned.1.call-done = f32[2304,64]{0,1:T(8,128)} async-done(((f32[2304,1024]{0,1:T(8,128)}), f32[2304,64]{0,1:T(8,128)}) %reduce-scatter.20.cloned.1.call-update) | async-done | bytes 589840 | tf_op jit(solution)/shard_map/reduce_scatter | solution.py:239
  (294 shorter events, 106.0 us)
Async XLA Ops:
  7.2 97.1 %copy-start.49 = (bf16[64,256]{1,0:T(8,128)(2,1)S(1)}, bf16[64,256]{1,0:T(8,128)(2,1)}, u32[]{:S(2)}) copy-start(bf16[64,256]{1,0:T(8,128)(2,1)} %param.22) | copy-start | bytes 98308
  7.2 140.7 %all-gather.6.cloned.1.call-start = ((), (), s32[]{:S(2)}) async-start(), calls=%async_computation.7 | async-start | bytes 1114112 | tf_op jit(solution)/shard_map/all_gather | solution.py:86
  7.9 183.8 %all-gather.8.cloned.1.call-start = ((), (), s32[]{:S(2)}) async-start(), calls=%async_computation.8 | async-start | bytes 1114112 | tf_op jit(solution)/shard_map/all_gather | solution.py:89
  8.7 213.1 %all-reduce.16.cloned.1.call-start = ((), (), s32[]{:S(2)}) async-start(), calls=%async_computation.9 | async-start | bytes 8388608 | tf_op jit(solution)/shard_map/psum | solution.py:149
  10.3 140.4 %copy-start.53 = (f32[64]{0:T(128)}, f32[64]{0:T(128)S(1)}, u32[]{:S(2)}) copy-start(f32[64]{0:T(128)S(1)} %convert_element_type.113) | copy-start | bytes 772
  58.2 89.7 %copy-start.45 = (f32[1024]{0:T(1024)}, f32[1024]{0:T(1024)S(1)}, u32[]{:S(2)}) copy-start(f32[1024]{0:T(1024)S(1)} %convert_element_type.111) | copy-start | bytes 12292
  58.2 86.9 %copy-start.8 = (bf16[1024,1024]{1,0:T(8,128)(2,1)S(1)}, bf16[1024,1024]{1,0:T(8,128)(2,1)}, u32[]{:S(2)}) copy-start(bf16[1024,1024]{1,0:T(8,128)(2,1)} %param.18) | copy-start | bytes 6291460
  60.5 43.8 %copy-start.43 = (f32[1024]{0:T(1024)}, f32[1024]{0:T(1024)S(1)}, u32[]{:S(2)}) copy-start(f32[1024]{0:T(1024)S(1)} %fusion.44) | copy-start | bytes 12292
  60.5 87.5 %copy-start.47 = (f32[1024]{0:T(1024)}, f32[1024]{0:T(1024)S(1)}, u32[]{:S(2)}) copy-start(f32[1024]{0:T(1024)S(1)} %fusion.53) | copy-start | bytes 12292
  61.9 84.7 %copy-start.51 = (f32[64]{0:T(128)}, f32[64]{0:T(128)S(1)}, u32[]{:S(2)}) copy-start(f32[64]{0:T(128)S(1)} %convert_element_type.116) | copy-start | bytes 772
  101.5 44.6 %copy-start.26 = (bf16[1024,256]{1,0:T(8,128)(2,1)}, bf16[1024,256]{1,0:T(8,128)(2,1)S(1)}, u32[]{:S(2)}) copy-start(bf16[1024,256]{1,0:T(8,128)(2,1)S(1)} %all_gather.29) | copy-start | bytes 1572868
  104.2 42.9 %copy-start.15 = (f32[1024,256]{0,1:T(8,128)}, f32[1024,256]{0,1:T(8,128)S(1)}, u32[]{:S(2)}) copy-start(f32[1024,256]{0,1:T(8,128)S(1)} %get-tuple-element.310) | copy-start | bytes 3145732
  104.2 42.9 %copy-start.41 = (f32[1024,4]{0,1:T(4,128)}, f32[1024,4]{0,1:T(4,128)S(1)}, u32[]{:S(2)}) copy-start(f32[1024,4]{0,1:T(4,128)S(1)} %get-tuple-element.309) | copy-start | bytes 49156
  104.3 42.8 %copy-start.35 = (f32[1024,4]{0,1:T(4,128)}, f32[1024,4]{0,1:T(4,128)S(1)}, u32[]{:S(2)}) copy-start(f32[1024,4]{0,1:T(4,128)S(1)} %fusion.52) | copy-start | bytes 49156
  196.5 25.2 %copy-start.9 = (bf16[1024,1024]{1,0:T(8,128)(2,1)S(1)}, bf16[1024,1024]{1,0:T(8,128)(2,1)}, u32[]{:S(2)}) copy-start(bf16[1024,1024]{1,0:T(8,128)(2,1)} %param.18) | copy-start | bytes 6291460
  196.6 109.9 %all-gather.10.cloned.1.call-start = ((), (), s32[]{:S(2)}) async-start(), calls=%async_computation.10 | async-start | bytes 5013504 | tf_op jit(solution)/shard_map/all_gather | solution.py:93
  197.1 191.4 %all-gather.12.cloned.1.call-start = ((), (), s32[]{:S(2)}) async-start(), calls=%async_computation.11 | async-start | bytes 5013504 | tf_op jit(solution)/shard_map/all_gather | solution.py:94
  197.7 273.0 %all-gather.14.cloned.1.call-start = ((), (), s32[]{:S(2)}) async-start(), calls=%async_computation.12 | async-start | bytes 5013504 | tf_op jit(solution)/shard_map/all_gather | solution.py:95
  198.3 331.6 %all-reduce.18.cloned.1.call-start = ((), (), s32[]{:S(2)}) async-start(), calls=%async_computation.13 | async-start | bytes 8388608 | tf_op jit(solution)/shard_map/psum | solution.py:168
  226.9 161.7 %copy-start.29 = (bf16[1024,1024]{1,0:T(8,128)(2,1)}, bf16[1024,1024]{1,0:T(8,128)(2,1)S(1)}, u32[]{:S(2)}) copy-start(bf16[1024,1024]{1,0:T(8,128)(2,1)S(1)} %multiply_convert_fusion.2) | copy-start | bytes 6291460
  502.7 309.7 %all-reduce.20.cloned.1.call-start = ((), (), s32[]{:S(2)}) async-start(), calls=%async_computation.21 | async-start | bytes 8388608 | tf_op jit(solution)/shard_map/psum | solution.py:155
  502.8 32.3 %copy-start.31 = (bf16[1024,1024]{1,0:T(8,128)(2,1)S(1)}, bf16[1024,1024]{1,0:T(8,128)(2,1)}, u32[]{:S(2)}) copy-start(bf16[1024,1024]{1,0:T(8,128)(2,1)} %param.31) | copy-start | bytes 6291460
  539.6 12.9 copy-start.18
  539.6 14.9 copy-start.37
  555.3 16.1 %slice-start = ((s8[16777216]{0:T(1024)(128)(4,1)}), s8[4194304]{0:T(1024)(128)(4,1)S(1)}, s32[]{:S(2)}) async-start(s8[16777216]{0:T(1024)(128)(4,1)} %bitcast.206), calls=%async_computation.22 | async-start | bytes 8388608 | tf_op jit(solution)/shard_map/while
  555.9 15.5 slice-start.1
  555.9 15.5 slice-start.2
  555.9 16.3 %slice-start.3 = ((s8[16777216]{0:T(1024)(128)(4,1)}), s8[4194304]{0:T(1024)(128)(4,1)S(1)}, s32[]{:S(2)}) async-start(s8[16777216]{0:T(1024)(128)(4,1)} %bitcast.206), calls=%async_computation.25 | async-start | bytes 8388608 | tf_op jit(solution)/shard_map/while
  581.6 13.9 slice-start.4
  599.6 20.6 %copy-start.19 = (bf16[1024,4,64]{0,2,1:T(8,128)(2,1)S(1)}, bf16[1024,4,64]{0,2,1:T(8,128)(2,1)}, u32[]{:S(2)}) copy-start(bf16[1024,4,64]{0,2,1:T(8,128)(2,1)} %copy-done.18) | copy-start | bytes 1572868 | tf_op jit(solution)/shard_map/while
  599.6 20.6 %copy-start.38 = (f32[2,4,2,512,1]{3,2,1,4,0:T(2,128)S(1)}, f32[2,4,2,512,1]{3,2,1,4,0:T(2,128)}, u32[]{:S(2)}) copy-start(f32[2,4,2,512,1]{3,2,1,4,0:T(2,128)} %copy-done.37) | copy-start | bytes 98308 | tf_op jit(solution)/shard_map/while
  620.3 14.9 copy-start.37
  635.9 16.1 %slice-start = ((s8[16777216]{0:T(1024)(128)(4,1)}), s8[4194304]{0:T(1024)(128)(4,1)S(1)}, s32[]{:S(2)}) async-start(s8[16777216]{0:T(1024)(128)(4,1)} %bitcast.206), calls=%async_computation.22 | async-start | bytes 8388608 | tf_op jit(solution)/shard_map/while
  636.5 15.6 slice-start.1
  636.5 15.5 slice-start.2
  636.5 16.3 %slice-start.3 = ((s8[16777216]{0:T(1024)(128)(4,1)}), s8[4194304]{0:T(1024)(128)(4,1)S(1)}, s32[]{:S(2)}) async-start(s8[16777216]{0:T(1024)(128)(4,1)} %bitcast.206), calls=%async_computation.25 | async-start | bytes 8388608 | tf_op jit(solution)/shard_map/while
  662.3 14.1 slice-start.4
  680.5 20.6 %copy-start.19 = (bf16[1024,4,64]{0,2,1:T(8,128)(2,1)S(1)}, bf16[1024,4,64]{0,2,1:T(8,128)(2,1)}, u32[]{:S(2)}) copy-start(bf16[1024,4,64]{0,2,1:T(8,128)(2,1)} %copy-done.18) | copy-start | bytes 1572868 | tf_op jit(solution)/shard_map/while
  680.5 20.6 %copy-start.38 = (f32[2,4,2,512,1]{3,2,1,4,0:T(2,128)S(1)}, f32[2,4,2,512,1]{3,2,1,4,0:T(2,128)}, u32[]{:S(2)}) copy-start(f32[2,4,2,512,1]{3,2,1,4,0:T(2,128)} %copy-done.37) | copy-start | bytes 98308 | tf_op jit(solution)/shard_map/while
  723.3 142.5 %reduce-scatter.10.cloned.1.call-start = ((), (), s32[]{:S(2)}) async-start(), calls=%async_computation.15 | async-start | bytes 1114112 | tf_op jit(solution)/shard_map/reduce_scatter | solution.py:234
  727.9 184.1 %reduce-scatter.12.cloned.1.call-start = ((), (), s32[]{:S(2)}) async-start(), calls=%async_computation.16 | async-start | bytes 1114112 | tf_op jit(solution)/shard_map/reduce_scatter | solution.py:235
  731.0 260.7 %reduce-scatter.8.cloned.1.call-start = ((), (), s32[]{:S(2)}) async-start(), calls=%async_computation.14 | async-start | bytes 2228224 | tf_op jit(solution)/shard_map/reduce_scatter | solution.py:233
  734.1 338.2 %reduce-scatter.14.cloned.1.call-start = ((), (), s32[]{:S(2)}) async-start(), calls=%async_computation.17 | async-start | bytes 2228224 | tf_op jit(solution)/shard_map/reduce_scatter | solution.py:236
  739.6 508.3 %reduce-scatter.16.cloned.1.call-start = ((), (), s32[]{:S(2)}) async-start(), calls=%async_computation.18 | async-start | bytes 10027008 | tf_op jit(solution)/shard_map/reduce_scatter | solution.py:237
  750.1 674.1 %reduce-scatter.18.cloned.1.call-start = ((), (), s32[]{:S(2)}) async-start(), calls=%async_computation.19 | async-start | bytes 10027008 | tf_op jit(solution)/shard_map/reduce_scatter | solution.py:238
  760.6 840.8 %reduce-scatter.20.cloned.1.call-start = ((), (), s32[]{:S(2)}) async-start(), calls=%async_computation.20 | async-start | bytes 10027008 | tf_op jit(solution)/shard_map/reduce_scatter | solution.py:239
  770.8 44.9 %copy-start.50 = (f32[1024]{0:T(1024)S(1)}, f32[1024]{0:T(1024)}, u32[]{:S(2)}) copy-start(f32[1024]{0:T(1024)} %get-tuple-element.230) | copy-start | bytes 12292
  770.8 87.4 %copy-start.44 = (f32[1024]{0:T(1024)S(1)}, f32[1024]{0:T(1024)}, u32[]{:S(2)}) copy-start(f32[1024]{0:T(1024)} %copy-done.43) | copy-start | bytes 12292
  (46 other events, 214.6 us)
Sparse Core Ops, SparseCore 0:
  10.8 58.8 all-gather.5
  72.5 56.3 all-gather.7
  196.7 24.9 all-reduce.15
  224.8 81.6 all-gather.9
  309.5 79.0 all-gather.11
  391.6 79.0 all-gather.13
  502.8 27.0 all-reduce.17
  723.4 29.6 all-reduce.19
  756.1 79.0 reduce-scatter.9
  837.9 74.1 reduce-scatter.11
  915.0 76.7 reduce-scatter.7
  994.5 77.6 reduce-scatter.13
  1079.4 168.4 reduce-scatter.15
  1254.0 170.1 reduce-scatter.17
  1431.3 170.0 reduce-scatter.19
where the time goes:
time: 1610 us
  waiting for transfers between devices  1000 us (62%)
  matrix products  230 us (14%)
  blocking collectives  207 us (13%)
  local copies, waits for them, and re-layouts  73.4 us (5%)
  other arithmetic  66.2 us (4%)
  between operations  16.5 us (1%)
    reduce_scatter x1, waiting for transfers between devices, local(): lax.psum_scatter(grad_down, 'fsdp', scatter_dimension=1, tiled=True)  177 us
    reduce_scatter x1, waiting for transfers between devices, local(): lax.psum_scatter(grad_up, 'fsdp', scatter_dimension=0, tiled=True)  176 us
    reduce_scatter x1, waiting for transfers between devices, local(): lax.psum_scatter(grad_gate, 'fsdp', scatter_dimension=0, tiled=True)  176 us
    unnamed x2, blocking collectives  85.7 us
    reduce_scatter x1, waiting for transfers between devices, local(): lax.psum_scatter(grad_output, 'fsdp', scatter_dimension=1, tiled=True)  80.5 us
    reduce_scatter x1, waiting for transfers between devices, local(): lax.psum_scatter(grad_query, 'fsdp', scatter_dimension=0, tiled=True)  79.7 us
    all_gather x1, waiting for transfers between devices, local(): lax.all_gather(w_gate, 'fsdp', axis=0, tiled=True)  79.5 us
    all_gather x1, waiting for transfers between devices, local(): lax.all_gather(w_down, 'fsdp', axis=1, tiled=True)  72.5 us
  transfers between devices with their start and end apart: 15, of which 11 were waited for; matrix products, arithmetic and copies ran while one was open for 9% of the time, Pallas kernels for 0%

commit v1 on v0

v1 whole, which is shorter than its diff:
```python
import functools

import jax
import jax.numpy as jnp
from jax import lax
from jax.experimental import pallas as pl
from jax.experimental.pallas import tpu as pltpu
from jax.sharding import PartitionSpec as P

HEAD_SIZE = 64
HALF = 32
QUERY_GROUP = 2
BLOCK = 256
MAXLEN = 512
EPS = 1e-05
THETA = 1000000.0
PAIR = 2
VMEM = 60 * 1024 * 1024


def root_mean_scale(value, gain):
    return value * lax.rsqrt(jnp.mean(value * value, axis=-1, keepdims=True) + EPS) * gain


def swish_product(gate, upward):
    return gate * jax.nn.sigmoid(gate) * upward


def matrix_product(left, right):
    return jnp.dot(left, right, preferred_element_type=jnp.float32)


def matmul_t(left, right):
    return lax.dot_general(
        left, right, (((1,), (1,)), ((), ())), preferred_element_type=jnp.float32
    )


def inner_rows(left, right):
    return lax.dot_general(
        left, right, (((0,), (0,)), ((), ())), preferred_element_type=jnp.float32
    )


def swap_halves(value):
    return jnp.concatenate([value[:, HALF:], value[:, :HALF]], axis=1)


def head(index):
    return slice(index * HEAD_SIZE, (index + 1) * HEAD_SIZE)


def normed_rotated(raw, gain, cosine, sine):
    n = raw * lax.rsqrt(jnp.mean(raw * raw, axis=-1, keepdims=True) + EPS) * gain
    return (n * cosine + swap_halves(n) * sine).astype(jnp.bfloat16)


def undo_norm(raw, gain, cosine, sine, d_out):
    d_n = d_out * cosine - swap_halves(d_out) * sine
    r = lax.rsqrt(jnp.mean(raw * raw, axis=-1, keepdims=True) + EPS)
    scaled = raw * r
    d_gain = jnp.sum(d_n * scaled, axis=0, keepdims=True)
    g_d = gain * d_n
    d_raw = r * (g_d - scaled * jnp.mean(g_d * scaled, axis=-1, keepdims=True))
    return d_raw.astype(jnp.bfloat16), d_gain


def probabilities(query, key, begin, row0, key0):
    scores = matmul_t(query, key) * (HEAD_SIZE ** -0.5)
    rows = row0 + lax.broadcasted_iota(jnp.int32, scores.shape, 0)
    cols = key0 + lax.broadcasted_iota(jnp.int32, scores.shape, 1)
    allowed = (cols <= rows) & (cols >= begin)
    scores = jnp.where(allowed, scores, -1e30)
    weights = jnp.exp(scores - jnp.max(scores, axis=-1, keepdims=True))
    return weights * (1.0 / jnp.sum(weights, axis=-1, keepdims=True))


def spans(rows):
    out = []
    for row0 in range(0, rows, BLOCK):
        key0 = max(0, row0 - MAXLEN)
        out.append((row0, key0, row0 + BLOCK - key0))
    return out


def forward_kernel(
    q_ref, k_ref, v_ref, cos_ref, sin_ref, begin_ref, gq_ref, gk_ref,
    att_ref, query_ref, key_ref, value_ref,
):
    rows = q_ref.shape[0]
    cosine, sine = cos_ref[...], sin_ref[...]
    value_ref[...] = v_ref[...].astype(jnp.bfloat16)
    for kv in range(PAIR):
        key_ref[:, head(kv)] = normed_rotated(k_ref[:, head(kv)], gk_ref[...], cosine, sine)
    for h in range(PAIR * QUERY_GROUP):
        query_ref[:, head(h)] = normed_rotated(q_ref[:, head(h)], gq_ref[...], cosine, sine)
    for row0, key0, width in spans(rows):
        begin = begin_ref[pl.ds(row0, BLOCK), :]
        for h in range(PAIR * QUERY_GROUP):
            kv = h // QUERY_GROUP
            prob = probabilities(
                query_ref[pl.ds(row0, BLOCK), head(h)],
                key_ref[pl.ds(key0, width), head(kv)],
                begin, row0, key0,
            ).astype(jnp.bfloat16)
            att_ref[pl.ds(row0, BLOCK), head(h)] = matrix_product(
                prob, value_ref[pl.ds(key0, width), head(kv)]
            ).astype(jnp.bfloat16)


def backward_kernel(
    q_ref, k_ref, query_ref, key_ref, value_ref, da_ref, cos_ref, sin_ref, begin_ref,
    gq_ref, gk_ref,
    dq_ref, dk_ref, dv_ref, dgq_ref, dgk_ref,
    key_acc, value_acc,
):
    rows = q_ref.shape[0]
    scale = HEAD_SIZE ** -0.5
    key_acc[...] = jnp.zeros_like(key_acc)
    value_acc[...] = jnp.zeros_like(value_acc)
    total_q = jnp.zeros((1, HEAD_SIZE), jnp.float32)
    total_k = jnp.zeros((1, HEAD_SIZE), jnp.float32)
    for row0, key0, width in spans(rows):
        block, keys = pl.ds(row0, BLOCK), pl.ds(key0, width)
        begin = begin_ref[block, :]
        for h in range(PAIR * QUERY_GROUP):
            kv = h // QUERY_GROUP
            query, key = query_ref[block, head(h)], key_ref[keys, head(kv)]
            d_out = da_ref[block, head(h)]
            prob = probabilities(query, key, begin, row0, key0)
            d_prob = matmul_t(d_out, value_ref[keys, head(kv)])
            delta = jnp.sum(d_prob * prob, axis=-1, keepdims=True)
            d_scores = (prob * (d_prob - delta)).astype(jnp.bfloat16)
            d_query = matrix_product(d_scores, key) * scale
            key_acc[kv, keys, :] += inner_rows(d_scores, query)
            value_acc[kv, keys, :] += inner_rows(prob.astype(jnp.bfloat16), d_out)
            d_raw, d_gain = undo_norm(
                q_ref[block, head(h)], gq_ref[...], cos_ref[block, :], sin_ref[block, :], d_query
            )
            dq_ref[block, head(h)] = d_raw
            total_q = total_q + d_gain
    for kv in range(PAIR):
        d_raw, d_gain = undo_norm(
            k_ref[:, head(kv)], gk_ref[...], cos_ref[...], sin_ref[...], key_acc[kv] * scale
        )
        dk_ref[:, head(kv)] = d_raw
        dv_ref[:, head(kv)] = value_acc[kv].astype(jnp.bfloat16)
        total_k = total_k + d_gain
    dgq_ref[...] = total_q[None]
    dgk_ref[...] = total_k[None]


def attention_forward(qkv, cosine, sine, begin, gain_q, gain_k, kv_heads):
    rows = qkv.shape[0]
    wide, narrow = PAIR * QUERY_GROUP * HEAD_SIZE, PAIR * HEAD_SIZE
    pairs = kv_heads // PAIR
    whole = lambda a: pl.BlockSpec(a.shape, lambda g: (0,) * a.ndim)
    q_cols = kv_heads * QUERY_GROUP * HEAD_SIZE // narrow
    k_cols = kv_heads * HEAD_SIZE // narrow
    q_spec = pl.BlockSpec((rows, wide), lambda g: (0, g))
    n_spec = pl.BlockSpec((rows, narrow), lambda g: (0, g))
    bf = jnp.bfloat16
    return pl.pallas_call(
        forward_kernel,
        grid=(pairs,),
        in_specs=[
            q_spec,
            pl.BlockSpec((rows, narrow), lambda g: (0, q_cols + g)),
            pl.BlockSpec((rows, narrow), lambda g: (0, q_cols + k_cols + g)),
            whole(cosine), whole(sine), whole(begin), whole(gain_q), whole(gain_k),
        ],
        out_specs=[q_spec, q_spec, n_spec, n_spec],
        out_shape=[
            jax.ShapeDtypeStruct((rows, wide * pairs), bf),
            jax.ShapeDtypeStruct((rows, wide * pairs), bf),
            jax.ShapeDtypeStruct((rows, narrow * pairs), bf),
            jax.ShapeDtypeStruct((rows, narrow * pairs), bf),
        ],
        compiler_params=pltpu.CompilerParams(vmem_limit_bytes=VMEM),
        cost_estimate=pl.CostEstimate(flops=6 * 10**9, bytes_accessed=10**7, transcendentals=5 * 10**6),
        name="attention_forward",
    )(qkv, qkv, qkv, cosine, sine, begin, gain_q, gain_k)


def attention_backward(qkv, query, key, value, d_att, cosine, sine, begin, gain_q, gain_k, kv_heads):
    rows = qkv.shape[0]
    wide, narrow = PAIR * QUERY_GROUP * HEAD_SIZE, PAIR * HEAD_SIZE
    pairs = kv_heads // PAIR
    whole = lambda a: pl.BlockSpec(a.shape, lambda g: (0,) * a.ndim)
    q_cols = kv_heads * QUERY_GROUP * HEAD_SIZE // narrow
    q_spec = pl.BlockSpec((rows, wide), lambda g: (0, g))
    n_spec = pl.BlockSpec((rows, narrow), lambda g: (0, g))
    g_spec = pl.BlockSpec((1, 1, HEAD_SIZE), lambda g: (g, 0, 0))
    bf = jnp.bfloat16
    return pl.pallas_call(
        backward_kernel,
        grid=(pairs,),
        in_specs=[
            q_spec,
            pl.BlockSpec((rows, narrow), lambda g: (0, q_cols + g)),
            q_spec, n_spec, n_spec, q_spec,
            whole(cosine), whole(sine), whole(begin), whole(gain_q), whole(gain_k),
        ],
        out_specs=[q_spec, n_spec, n_spec, g_spec, g_spec],
        out_shape=[
            jax.ShapeDtypeStruct((rows, wide * pairs), bf),
            jax.ShapeDtypeStruct((rows, narrow * pairs), bf),
            jax.ShapeDtypeStruct((rows, narrow * pairs), bf),
            jax.ShapeDtypeStruct((pairs, 1, HEAD_SIZE), jnp.float32),
            jax.ShapeDtypeStruct((pairs, 1, HEAD_SIZE), jnp.float32),
        ],
        scratch_shapes=[
            pltpu.VMEM((PAIR, rows, HEAD_SIZE), jnp.float32),
            pltpu.VMEM((PAIR, rows, HEAD_SIZE), jnp.float32),
        ],
        compiler_params=pltpu.CompilerParams(vmem_limit_bytes=VMEM),
        cost_estimate=pl.CostEstimate(flops=2 * 10**10, bytes_accessed=10**7, transcendentals=5 * 10**6),
        name="attention_backward",
    )(qkv, qkv, query, key, value, d_att, cosine, sine, begin, gain_q, gain_k)


def pair_sum(value):
    return value + lax.ppermute(value, "tensor", [(0, 1), (1, 0)])


def local(
    tokens,
    lengths,
    w_query,
    key_weight,
    value_weight,
    w_output,
    w_gate,
    w_up,
    w_down,
    gain_attn,
    gain_ffn,
    gain_query,
    key_norm_gain,
    cotangent,
):
    bf, f32 = jnp.bfloat16, jnp.float32
    rows, width = tokens.shape
    part = w_query.shape[0]
    q_width, kv_width, ff = w_query.shape[1], key_weight.shape[1], w_gate.shape[1]
    kv_heads = kv_width // HEAD_SIZE
    qkv_width = q_width + 2 * kv_width

    gains = jnp.pad(jnp.stack([gain_attn, gain_ffn], axis=1), ((0, 0), (0, 126)))
    attn_pack = jnp.concatenate(
        [w_query, key_weight, value_weight, w_output.T, gains], axis=1
    )
    ffn_pack = jnp.concatenate([w_gate, w_up, w_down.T], axis=1)
    attn_all = lax.all_gather(attn_pack, "fsdp", axis=0, tiled=True)
    attn_all, ffn_pack = lax.optimization_barrier((attn_all, ffn_pack))
    ffn_all = lax.all_gather(ffn_pack, "fsdp", axis=0, tiled=True)
    qkv_all = attn_all[:, :qkv_width]
    output_t = attn_all[:, qkv_width : qkv_width + q_width]
    first_gain = attn_all[:, qkv_width + q_width].astype(f32)
    second_gain = attn_all[:, qkv_width + q_width + 1].astype(f32)
    query_gain = gain_query.astype(f32)[None]
    key_gain = key_norm_gain.astype(f32)[None]

    lens = lengths[0]
    ends = jnp.cumsum(lens)
    row_ids = jnp.arange(rows, dtype=jnp.int32)
    passed = row_ids[:, None] >= ends[None, :]
    begin = jnp.sum(jnp.where(passed, lens[None, :], 0), axis=1)
    position = (row_ids - begin).astype(f32)
    freq = THETA ** (-jnp.arange(HALF, dtype=f32) * 2.0 / HEAD_SIZE)
    angle = position[:, None] * freq[None, :]
    cosine, sine = jnp.cos(angle), jnp.sin(angle)
    cosine = jnp.concatenate([cosine, cosine], axis=1)
    sine = jnp.concatenate([-sine, sine], axis=1)
    begin = begin[:, None]

    x_float = tokens.astype(f32)
    h1 = root_mean_scale(x_float, first_gain).astype(bf)
    qkv = matrix_product(h1, qkv_all)
    attended, query, key, value = attention_forward(
        qkv, cosine, sine, begin, query_gain, key_gain, kv_heads
    )
    resid = x_float + pair_sum(matmul_t(attended, output_t))
    h2 = root_mean_scale(resid, second_gain).astype(bf)

    gate = matrix_product(h2, ffn_all[:, :ff])
    upward = matrix_product(h2, ffn_all[:, ff : 2 * ff])
    down_t = ffn_all[:, 2 * ff :]
    d_hidden = matrix_product(cotangent, down_t)
    hidden, pull_swish = jax.vjp(swish_product, gate, upward)
    d_gate, d_up = pull_swish(d_hidden)
    hidden = hidden.astype(bf)
    d_both = jnp.concatenate([d_gate.astype(bf), d_up.astype(bf)], axis=1)
    d_second = pair_sum(matmul_t(d_both, ffn_all[:, : 2 * ff]))
    grad_both = inner_rows(h2, d_both).astype(bf)
    grad_down = inner_rows(cotangent, hidden).astype(bf)
    ffn_grads = lax.psum_scatter(
        jnp.concatenate([grad_both, grad_down], axis=1), "fsdp", scatter_dimension=0, tiled=True
    )
    ffn_out = pair_sum(matmul_t(hidden, down_t).astype(bf)).astype(f32)
    layer_out = (resid + ffn_out).astype(bf)

    unused_norm, pull_second = jax.vjp(root_mean_scale, resid, second_gain)
    d_resid_norm, grad_second_gain = pull_second(d_second)
    d_resid = cotangent.astype(f32) + d_resid_norm
    d_branch = d_resid.astype(bf)
    d_attended = matrix_product(d_branch, output_t).astype(bf)
    d_q, d_k, d_v, gain_q_part, gain_k_part = attention_backward(
        qkv, query, key, value, d_attended, cosine, sine, begin, query_gain, key_gain, kv_heads
    )
    d_qkv = jnp.concatenate([d_q, d_k, d_v], axis=1)
    grad_qkv = inner_rows(h1, d_qkv).astype(bf)
    grad_out = inner_rows(d_branch, attended).astype(bf)
    attn_grads = lax.psum_scatter(
        jnp.concatenate([grad_qkv, grad_out], axis=1), "fsdp", scatter_dimension=0, tiled=True
    )
    d_first = pair_sum(matmul_t(d_qkv, qkv_all).astype(bf)).astype(f32)
    unused_first, pull_first = jax.vjp(root_mean_scale, x_float, first_gain)
    d_x_norm, grad_first_gain = pull_first(d_first)
    token_grad = (d_resid + d_x_norm).astype(bf)

    small = jnp.concatenate(
        [
            grad_first_gain * 0.5,
            grad_second_gain * 0.5,
            jnp.sum(gain_q_part, axis=(0, 1)),
            jnp.sum(gain_k_part, axis=(0, 1)),
        ]
    )
    small = lax.psum(small, ("fsdp", "tensor"))
    start = lax.axis_index("fsdp") * part
    shard_first = lax.dynamic_slice_in_dim(small, start, part, 0)
    shard_second = lax.dynamic_slice_in_dim(small, width + start, part, 0)
    gain_q_grad = small[2 * width : 2 * width + HEAD_SIZE]
    gain_k_grad = small[2 * width + HEAD_SIZE :]

    attn_grads = attn_grads.astype(f32)
    ffn_grads = ffn_grads.astype(f32)
    return (
        layer_out,
        token_grad,
        attn_grads[:, :q_width],
        attn_grads[:, q_width : q_width + kv_width],
        attn_grads[:, q_width + kv_width : qkv_width],
        attn_grads[:, qkv_width:].T,
        ffn_grads[:, :ff],
        ffn_grads[:, ff : 2 * ff],
        ffn_grads[:, 2 * ff :].T,
        shard_first,
        shard_second,
        gain_q_grad,
        gain_k_grad,
    )


def solution(mesh):
    return jax.shard_map(
        local,
        mesh=mesh,
        in_specs=(
            P("fsdp", None),
            P("fsdp", None),
            P("fsdp", "tensor"),
            P("fsdp", "tensor"),
            P("fsdp", "tensor"),
            P("tensor", "fsdp"),
            P("fsdp", "tensor"),
            P("fsdp", "tensor"),
            P("tensor", "fsdp"),
            P("fsdp"),
            P("fsdp"),
            P(),
            P(),
            P("fsdp", None),
        ),
        out_specs=(
            P("fsdp", None),
            P("fsdp", None),
            P("fsdp", "tensor"),
            P("fsdp", "tensor"),
            P("fsdp", "tensor"),
            P("tensor", "fsdp"),
            P("fsdp", "tensor"),
            P("fsdp", "tensor"),
            P("tensor", "fsdp"),
            P("fsdp"),
            P("fsdp"),
            P(),
            P(),
        ),
        check_vma=False,
    )
```

time: 1610 us -> 778 us (0.48)
  waiting for transfers between devices: 1000 us -> 433 us
  blocking collectives: 207 us -> 38.6 us
  matrix products: 230 us -> 110 us
  Pallas kernels: 0 us -> 87.2 us
  local copies, waits for them, and re-layouts: 73.4 us -> 40.5 us
  other arithmetic: 66.2 us -> 48 us
    reduce_scatter x7 -> x1, waiting for transfers between devices: 736 us -> 222 us  [local(): lax.psum_scatter(jnp.concatenate([grad_both, grad_down], axis=1), 'fsdp',...]
    dot_general x14 -> x0, matrix products: 101 us -> none  [the longest x4 38.9 us: block_scores(): jnp.einsum('bkgd,skd->kgbs', query_block_slice, key_rows, preferred_eleme...]
    pallas_call x0 -> x2, Pallas kernels: none -> 87.2 us  [the longest x1 50.5 us: attention_backward(): pl.pallas_call(backward_kernel, grid=(pairs,), in_specs=[q_spec, pl.Block...]
    unnamed x2 -> x0, blocking collectives: 85.7 us -> none
    all_gather x2 -> x0, blocking collectives: 80.4 us -> none  [the longest x1 40.8 us: local(): lax.all_gather(value_weight, 'fsdp', axis=0, tiled=True)]
    all_gather x5 -> x2, waiting for transfers between devices: 224 us -> 174 us  [the longest x1 103 us: local(): ffn_all = lax.all_gather(ffn_pack, 'fsdp', axis=0, tiled=True)]
    dynamic_update_slice x8 -> x0, local copies, waits for them, and re-layouts: 43.3 us -> none  [local(): attended_blocks, log_totals = lax.map(forward_block, starts)]
    psum x3 -> x0, waiting for transfers between devices: 40.5 us -> none  [the longest x1 22.9 us: local(): branch = lax.psum(matrix_product(attended, output_all), 'tensor')]
  transfers between devices with their start and end apart: 15 -> 8, of which waited for: 11 -> 6; matrix products, arithmetic and copies ran while one was open for 9% -> 14% of each run, Pallas kernels for 0% -> 5%
where the time goes in v1:
time: 778 us; the launch traced here: 772 us
  waiting for transfers between devices  433 us (56%)
  matrix products  110 us (14%)
  Pallas kernels  87.2 us (11%)
  other arithmetic  48 us (6%)
  local copies, waits for them, and re-layouts  40.5 us (5%)
  blocking collectives  38.6 us (5%)
  between operations  14.3 us (2%)
    reduce_scatter x1, waiting for transfers between devices, local(): lax.psum_scatter(jnp.concatenate([grad_both, grad_down], axis=1), 'fsdp',...  222 us
    all_gather x1, waiting for transfers between devices, local(): ffn_all = lax.all_gather(ffn_pack, 'fsdp', axis=0, tiled=True)  103 us
    all_gather x1, waiting for transfers between devices, local(): attn_all = lax.all_gather(attn_pack, 'fsdp', axis=0, tiled=True)  71 us
    pallas_call x1, Pallas kernels, attention_backward(): pl.pallas_call(backward_kernel, grid=(pairs,), in_specs=[q_spec, pl.Block...  50.5 us
    dot_general x5, matrix products, matrix_product(): return jnp.dot(left, right, preferred_element_type=jnp.float32)  46.6 us
    psum x1, blocking collectives, local(): small = lax.psum(small, ('fsdp', 'tensor'))  38.6 us
    pallas_call x1, Pallas kernels, attention_forward(): pl.pallas_call(forward_kernel, grid=(pairs,), in_specs=[q_spec, pl.BlockS...  36.7 us
    unnamed x59, local copies, waits for them, and re-layouts  35.7 us
  transfers between devices with their start and end apart: 8, of which 6 were waited for; matrix products, arithmetic and copies ran while one was open for 14% of the time, Pallas kernels for 5%

profile of v1, /device:TPU:0, one launch (start us, length us, event | category | flops | bytes accessed | tf_op | source)
XLA Modules:
  0.0 771.6 jit_solution(15881068552084906542)
XLA Ops:
  12.0 2.1 pad_maximum_fusion.5
  14.1 71.0 %all-gather.3.cloned.1.call-done = bf16[1024,1664]{1,0:T(8,128)(2,1)} async-done(((bf16[64,1664]{1,0:T(8,128)(2,1)}), bf16[1024,1664]{1,0:T(8,128)(2,1)}) %all-gather.3.cloned.1.call-update) | async-done | bytes 3407888 | tf_op jit(solution)/shard_map/all_gather | solution.py:254
  85.2 2.9 copy.93
  88.4 1.0 copy.96.begin_ref
  89.4 1.9 fusion.38
  91.3 1.3 pad_maximum_fusion.6
  94.6 4.5 fusion.29.q_ref.k_ref.v_ref
  99.1 36.7 %attention_forward.1 = (bf16[1024,512]{1,0:T(8,128)(2,1)}, bf16[1024,512]{1,0:T(8,128)(2,1)}, bf16[1024,256]{1,0:T(8,128)(2,1)}, bf16[1024,256]{1,0:T(8,128)(2,1)}) custom-call(f32[1024,1024]{1,0:T(8,128)} %fusion.29.q_ref.k_ref.v_ref, f32[1024,1024]{1,0:T(8,128)} %fusion.29.q_ref.k_ref.v_ref, f32[1024,1024]{1,0:T(8,128)} %fusion.29.q_ref.k_ref.v_ref, ...), custom_call_target="tpu_custom_call" | custom-call | flops 6000000000 | bytes 10000000 | tf_op jit(solution)/shard_map/attention_forward/pallas_call | solution.py:163
  135.8 2.8 fusion.34
  138.7 7.1 collective-permute-done
  145.8 1.7 multiply_reduce_fusion.2
  147.5 2.0 copy-done
  149.6 1.7 multiply_convert_fusion.1
  151.3 102.6 %all-gather.5.cloned.1.call-done = bf16[1024,6912]{1,0:T(8,128)(2,1)} async-done(((bf16[64,6912]{1,0:T(8,128)(2,1)}), bf16[1024,6912]{1,0:T(8,128)(2,1)}) %all-gather.5.cloned.1.call-update) | async-done | bytes 14155792 | tf_op jit(solution)/shard_map/all_gather | solution.py:256
  253.9 10.3 %fusion.10 = f32[1024,2304]{1,0:T(8,128)} fusion(bf16[1024,1024]{0,1:T(8,128)(2,1)} %multiply_convert_fusion.1, bf16[1024,6912]{1,0:T(8,128)(2,1)} %all-gather.5.cloned.1.call-done), kind=kOutput, calls=%fused_computation.28 | convolution fusion | flops 4831838208 | bytes 16252928 | tf_op jit(solution)/shard_map/dot_general | solution.py:30
  264.2 9.9 %fusion.21 = f32[2304,1024]{0,1:T(8,128)} fusion(bf16[1024,1024]{1,0:T(8,128)(2,1)S(1)} %copy-done.7, bf16[1024,6912]{1,0:T(8,128)(2,1)} %all-gather.5.cloned.1.call-done), kind=kOutput, calls=%fused_computation.44 | convolution fusion | flops 4831838208 | bytes 16252928 | tf_op jit(solution)/shard_map/dot_general | solution.py:30
  274.1 17.5 %fusion.2 = (bf16[1024,2304]{1,0:T(8,128)(2,1)}, bf16[1024,2304]{1,0:T(8,128)(2,1)}, bf16[1024,2304]{1,0:T(8,128)(2,1)}) fusion(f32[1024,2304]{1,0:T(8,128)} %fusion.10, f32[2304,1024]{0,1:T(8,128)} %fusion.21, bf16[1024,1024]{0,1:T(8,128)(2,1)S(1)} %copy-done.8, bf16[1024,6912]{1,0:T(8,128)(2,1)} %all-gather.5.cloned.1.call-done), kind=kOutput, calls=%fused_computation.5 | convolution fusion | flops 4869586944 | bytes 39845888 | tf_op jit(solution)/shard_map/dot_general | solution.py:30
  291.6 16.8 %fusion.3 = f32[1024,1024]{0,1:T(8,128)} fusion(bf16[1024,6912]{1,0:T(8,128)(2,1)} %all-gather.5.cloned.1.call-done, bf16[1024,2304]{1,0:T(8,128)(2,1)} %get-tuple-element.109, bf16[1024,2304]{1,0:T(8,128)(2,1)} %get-tuple-element.108), kind=kOutput, calls=%fused_computation.6 | convolution fusion | flops 9682550784 | bytes 23068672 | tf_op jit(solution)/shard_map/dot_general | solution.py:34
  308.4 9.3 %fusion.25 = bf16[1024,1024]{0,1:T(8,128)(2,1)} fusion(bf16[1024,2304]{1,0:T(8,128)(2,1)} %get-tuple-element.110, bf16[1024,6912]{1,0:T(8,128)(2,1)} %all-gather.5.cloned.1.call-done), kind=kOutput, calls=%fused_computation.49 | convolution fusion | flops 4832886784 | bytes 11534336 | tf_op jit(solution)/shard_map/dot_general | solution.py:34
  318.2 3.9 copy.98
  322.1 6.1 multiply_reduce_fusion
  328.3 1.0 copy-done.4
  329.8 5.9 fusion.16
  335.7 4.5 convolution_convert_fusion.5.da_ref
  340.2 1.3 convolution_convert_fusion.4
  341.5 50.5 %attention_backward.1 = (bf16[1024,512]{1,0:T(8,128)(2,1)}, bf16[1024,256]{1,0:T(8,128)(2,1)}, bf16[1024,256]{1,0:T(8,128)(2,1)}, f32[2,1,64]{2,1,0:T(1,128)}, f32[2,1,64]{2,1,0:T(1,128)}) custom-call(f32[1024,1024]{1,0:T(8,128)} %fusion.29.q_ref.k_ref.v_ref, f32[1024,1024]{1,0:T(8,128)} %fusion.29.q_ref.k_ref.v_ref, ...), custom_call_target="tpu_custom_call" | custom-call | flops 20000000000 | bytes 10000000 | tf_op jit(solution)/shard_map/attention_backward/pallas_call | solution.py:195
  392.0 1.3 constant_dynamic-update-slice_fusion.6
  393.3 1.1 constant_dynamic-update-slice_fusion.5
  394.4 1.1 constant_dynamic-update-slice_fusion.4
  395.6 1.3 copy-done.12
  396.9 2.6 convolution_convert_fusion.2
  399.5 1.9 pad_maximum_fusion.4
  401.4 4.6 copy.116
  406.2 8.1 %fusion.9 = bf16[1024,2304]{1,0:T(8,128)(2,1)S(1)} fusion(bf16[1024,2304]{1,0:T(8,128)(2,1)} %get-tuple-element.110, bf16[1024,1024]{1,0:T(8,128)(2,1)} %param.27), kind=kOutput, calls=%fused_computation.27 | convolution fusion | flops 4834197504 | bytes 11534336 | tf_op jit(solution)/shard_map/dot_general | solution.py:40
  414.3 16.1 %convolution_convert_fusion = bf16[1024,4608]{1,0:T(8,128)(2,1)} fusion(bf16[1024,1024]{0,1:T(8,128)(2,1)S(1)} %copy-done.9, bf16[1024,2304]{1,0:T(8,128)(2,1)} %get-tuple-element.109, bf16[1024,2304]{1,0:T(8,128)(2,1)} %get-tuple-element.108), kind=kOutput, calls=%fused_computation.2 | convolution fusion | flops 9687269376 | bytes 20971520 | tf_op jit(solution)/shard_map/dot_general | solution.py:40
  430.4 12.4 %pad_maximum_fusion = bf16[1024,6912]{1,0:T(8,128)(2,1)} fusion(bf16[1024,2304]{1,0:T(8,128)(2,1)S(1)} %fusion.9, bf16[1024,4608]{1,0:T(8,128)(2,1)} %convolution_convert_fusion), kind=kLoop, calls=%fused_computation | loop fusion | flops 28311552 | bytes 28311552 | tf_op jit(solution)/shard_map/concatenate | solution.py:298
  442.8 6.0 convolution_convert_fusion.3
  448.9 4.1 copy.105
  453.3 4.2 fusion.15
  457.5 5.0 fusion.18
  462.6 4.0 copy.106
  466.6 38.6 %psum.7 = f32[2176]{0:T(1024)S(1)} all-reduce(f32[2176]{0:T(1024)S(1)} %concatenate.35), channel_id=1, replica_groups=mesh['fsdp'=16,'tensor'=2] {'fsdp','tensor'}, use_global_device_ids=true, to_apply=%region_12.13 | all-reduce | flops 2176 | bytes 17408 | tf_op jit(solution)/shard_map/psum | solution.py:330
  505.7 29.7 %reduce-scatter.7.cloned.1.call-done = bf16[64,1536]{1,0:T(8,128)(2,1)} async-done(((bf16[1024,1536]{1,0:T(8,128)(2,1)}), bf16[64,1536]{1,0:T(8,128)(2,1)}) %reduce-scatter.7.cloned.1.call-update) | async-done | bytes 196624
  535.4 1.1 copy.117
  539.7 221.9 %reduce-scatter.5.cloned.1.call-done = bf16[64,6912]{1,0:T(8,128)(2,1)} async-done(((bf16[1024,6912]{1,0:T(8,128)(2,1)}), bf16[64,6912]{1,0:T(8,128)(2,1)}) %reduce-scatter.5.cloned.1.call-update) | async-done | bytes 884752 | tf_op jit(solution)/shard_map/reduce_scatter | solution.py:297
  761.6 1.4 convert_element_type.123
  762.9 0.9 slice_bitcast_fusion
  763.8 1.1 fusion.43
  (86 shorter events, 12.5 us)
Async XLA Ops:
  7.2 80.9 %copy-start.18 = (s32[1,8]{1,0:T(1,128)S(1)}, s32[1,8]{1,0:T(1,128)}, u32[]{:S(2)}) copy-start(s32[1,8]{1,0:T(1,128)} %param.15) | copy-start | bytes 100
  7.2 78.0 %all-gather.3.cloned.1.call-start = ((), (), s32[]{:S(2)}) async-start(), calls=%async_computation.2 | async-start | bytes 3620864 | tf_op jit(solution)/shard_map/all_gather | solution.py:254
  11.3 0.7 copy-start.13
  12.0 242.0 %all-gather.5.cloned.1.call-start = ((), (), s32[]{:S(2)}) async-start(), calls=%async_computation.3 | async-start | bytes 15040512 | tf_op jit(solution)/shard_map/all_gather | solution.py:256
  85.2 7.5 copy-start.19
  85.2 7.5 copy-start.20
  85.2 450.2 %reduce-scatter.7.cloned.1.call-start = ((), (), s32[]{:S(2)}) async-start(), calls=%async_computation.5 | async-start | bytes 3342336
  89.4 4.8 copy-start.11
  93.7 0.6 copy-start.14
  138.6 7.2 collective-permute-start
  147.5 2.1 copy-start
  253.9 10.3 %copy-start.7 = (bf16[1024,1024]{1,0:T(8,128)(2,1)S(1)}, bf16[1024,1024]{1,0:T(8,128)(2,1)}, u32[]{:S(2)}) copy-start(bf16[1024,1024]{1,0:T(8,128)(2,1)} %param.27) | copy-start | bytes 6291460
  264.2 9.9 %copy-start.8 = (bf16[1024,1024]{0,1:T(8,128)(2,1)S(1)}, bf16[1024,1024]{0,1:T(8,128)(2,1)}, u32[]{:S(2)}) copy-start(bf16[1024,1024]{0,1:T(8,128)(2,1)} %multiply_convert_fusion.1) | copy-start | bytes 6291460
  308.4 13.8 %collective-permute-start.2 = (f32[1024,1024]{0,1:T(8,128)}, f32[1024,1024]{0,1:T(8,128)}, u32[]{:S(2)}, u32[]{:S(2)}) collective-permute-start(f32[1024,1024]{0,1:T(8,128)} %fusion.3), channel_id=1, source_target_pairs={{0,1},{1,0},{2,3},{3,2},{4,5},{5,4},{6,7},{7,6},{8,9},{9,8},{10,11... | collective-permute-start | bytes 12582920 | tf_op jit(solution)/shard_map/ppermute | solution.py:223
  317.7 10.5 %collective-permute-start.1 = (bf16[1024,1024]{0,1:T(8,128)(2,1)}, bf16[1024,1024]{0,1:T(8,128)(2,1)}, u32[]{:S(2)}, u32[]{:S(2)}) collective-permute-start(bf16[1024,1024]{0,1:T(8,128)(2,1)} %fusion.25), channel_id=1, source_target_pairs={{0,1},{1,0},{2,3},{3,2},{4,5},{5,4},{6,7},{7,6},{8,9},{9,8},{10,11... | collective-permute-start | bytes 6291464 | tf_op jit(solution)/shard_map/ppermute | solution.py:223
  322.1 6.1 copy-start.1
  322.1 7.1 copy-start.4
  322.1 7.7 copy-start.5
  335.7 4.5 copy-start.2
  335.7 4.5 copy-start.10
  395.5 1.3 copy-start.12
  406.1 355.5 %reduce-scatter.5.cloned.1.call-start = ((), (), s32[]{:S(2)}) async-start(), calls=%async_computation.4 | async-start | bytes 15040512 | tf_op jit(solution)/shard_map/reduce_scatter | solution.py:297
  406.1 8.2 %copy-start.9 = (bf16[1024,1024]{0,1:T(8,128)(2,1)S(1)}, bf16[1024,1024]{0,1:T(8,128)(2,1)}, u32[]{:S(2)}) copy-start(bf16[1024,1024]{0,1:T(8,128)(2,1)} %multiply_convert_fusion.1) | copy-start | bytes 6291460
  442.8 6.0 copy-start.17
  442.8 6.0 copy-start.16
  448.8 4.5 collective-permute-start.3
  453.0 4.5 copy-start.15
  453.0 4.5 copy-start.3
  761.6 2.2 copy-start.6
Sparse Core Ops, SparseCore 0:
  12.1 73.0 all-gather.2
  88.5 165.3 all-gather.4
  406.2 129.1 reduce-scatter.6
  541.0 220.4 reduce-scatter.4

commit v2 on v1

--- a/solution.py
+++ b/solution.py
@@ -294,9 +294,9 @@
     d_second = pair_sum(matmul_t(d_both, ffn_all[:, : 2 * ff]))
     grad_both = inner_rows(h2, d_both).astype(bf)
     grad_down = inner_rows(cotangent, hidden).astype(bf)
-    ffn_grads = lax.psum_scatter(
-        jnp.concatenate([grad_both, grad_down], axis=1), "fsdp", scatter_dimension=0, tiled=True
-    )
+    ffn_packed = jnp.concatenate([grad_both, grad_down], axis=1)
+    ffn_packed, d_second = lax.optimization_barrier((ffn_packed, d_second))
+    ffn_grads = lax.psum_scatter(ffn_packed, "fsdp", scatter_dimension=0, tiled=True)
     ffn_out = pair_sum(matmul_t(hidden, down_t).astype(bf)).astype(f32)
     layer_out = (resid + ffn_out).astype(bf)
 
@@ -311,9 +311,9 @@
     d_qkv = jnp.concatenate([d_q, d_k, d_v], axis=1)
     grad_qkv = inner_rows(h1, d_qkv).astype(bf)
     grad_out = inner_rows(d_branch, attended).astype(bf)
-    attn_grads = lax.psum_scatter(
-        jnp.concatenate([grad_qkv, grad_out], axis=1), "fsdp", scatter_dimension=0, tiled=True
-    )
+    attn_packed = jnp.concatenate([grad_qkv, grad_out], axis=1)
+    attn_packed, ffn_grads = lax.optimization_barrier((attn_packed, ffn_grads))
+    attn_grads = lax.psum_scatter(attn_packed, "fsdp", scatter_dimension=0, tiled=True)
     d_first = pair_sum(matmul_t(d_qkv, qkv_all).astype(bf)).astype(f32)
     unused_first, pull_first = jax.vjp(root_mean_scale, x_float, first_gain)
     d_x_norm, grad_first_gain = pull_first(d_first)

time: 778 us -> 720 us (0.925)
  waiting for transfers between devices: 433 us -> 376 us
    reduce_scatter x1, waiting for transfers between devices: 222 us -> 131 us  [local(): lax.psum_scatter(ffn_packed, 'fsdp', scatter_dimension=0, tiled=True)]
    unnamed x5, waiting for transfers between devices: 29.7 us -> 64.4 us
    unnamed x59 -> x69, local copies, waits for them, and re-layouts: 35.7 us -> 33.2 us
  transfers between devices with their start and end apart: 8 -> 8, of which waited for: 6 -> 6; matrix products, arithmetic and copies ran while one was open for 14% -> 16% of each run, Pallas kernels for 5% -> 12%
where the time goes in v2:
time: 720 us; the launch traced here: 714 us
  waiting for transfers between devices  376 us (52%)
  matrix products  109 us (15%)
  Pallas kernels  87.3 us (12%)
  other arithmetic  48.4 us (7%)
  blocking collectives  40.5 us (6%)
  local copies, waits for them, and re-layouts  38.4 us (5%)
  between operations  14.4 us (2%)
    reduce_scatter x1, waiting for transfers between devices, local(): lax.psum_scatter(ffn_packed, 'fsdp', scatter_dimension=0, tiled=True)  131 us
    all_gather x1, waiting for transfers between devices, local(): ffn_all = lax.all_gather(ffn_pack, 'fsdp', axis=0, tiled=True)  102 us
    all_gather x1, waiting for transfers between devices, local(): attn_all = lax.all_gather(attn_pack, 'fsdp', axis=0, tiled=True)  71 us
    unnamed x5, waiting for transfers between devices  64.4 us
    pallas_call x1, Pallas kernels, attention_backward(): pl.pallas_call(backward_kernel, grid=(pairs,), in_specs=[q_spec, pl.Block...  50.7 us
    dot_general x5, matrix products, matrix_product(): return jnp.dot(left, right, preferred_element_type=jnp.float32)  46.6 us
    psum x1, blocking collectives, local(): small = lax.psum(small, ('fsdp', 'tensor'))  40.5 us
    pallas_call x1, Pallas kernels, attention_forward(): pl.pallas_call(forward_kernel, grid=(pairs,), in_specs=[q_spec, pl.BlockS...  36.6 us
  transfers between devices with their start and end apart: 8, of which 6 were waited for; matrix products, arithmetic and copies ran while one was open for 16% of the time, Pallas kernels for 12%

profile of v2, /device:TPU:0, one launch (start us, length us, event | category | flops | bytes accessed | tf_op | source)
XLA Modules:
  0.0 714.0 jit_solution(13432832259018227184)
XLA Ops:
  7.2 0.8 constant_dynamic-update-slice_fusion.3
  12.0 2.1 pad_maximum_fusion.5
  14.1 71.0 %all-gather.3.cloned.1.call-done = bf16[1024,1664]{1,0:T(8,128)(2,1)} async-done(((bf16[64,1664]{1,0:T(8,128)(2,1)}), bf16[1024,1664]{1,0:T(8,128)(2,1)}) %all-gather.3.cloned.1.call-update) | async-done | bytes 3407888 | tf_op jit(solution)/shard_map/all_gather | solution.py:254
  85.2 2.9 copy.93
  88.4 1.2 copy.96.begin_ref
  89.6 1.9 fusion.38
  91.5 1.3 pad_maximum_fusion.6
  94.8 4.5 fusion.29.q_ref.k_ref.v_ref
  99.3 36.6 %attention_forward.1 = (bf16[1024,512]{1,0:T(8,128)(2,1)}, bf16[1024,512]{1,0:T(8,128)(2,1)}, bf16[1024,256]{1,0:T(8,128)(2,1)}, bf16[1024,256]{1,0:T(8,128)(2,1)}) custom-call(f32[1024,1024]{1,0:T(8,128)} %fusion.29.q_ref.k_ref.v_ref, f32[1024,1024]{1,0:T(8,128)} %fusion.29.q_ref.k_ref.v_ref, f32[1024,1024]{1,0:T(8,128)} %fusion.29.q_ref.k_ref.v_ref, ...), custom_call_target="tpu_custom_call" | custom-call | flops 6000000000 | bytes 10000000 | tf_op jit(solution)/shard_map/attention_forward/pallas_call | solution.py:163
  135.9 2.8 fusion.34
  138.8 7.1 %collective-permute-done = f32[1024,1024]{0,1:T(8,128)S(1)} collective-permute-done((f32[1024,1024]{0,1:T(8,128)S(1)}, f32[1024,1024]{0,1:T(8,128)S(1)}, u32[]{:S(2)}, u32[]{:S(2)}) %collective-permute-start) | collective-permute-done | bytes 4194336 | tf_op jit(solution)/shard_map/ppermute | solution.py:223
  146.0 1.7 multiply_reduce_fusion.2
  147.7 2.0 copy-done
  149.7 1.7 multiply_convert_fusion.1
  151.5 101.9 %all-gather.5.cloned.1.call-done = bf16[1024,6912]{1,0:T(8,128)(2,1)} async-done(((bf16[64,6912]{1,0:T(8,128)(2,1)}), bf16[1024,6912]{1,0:T(8,128)(2,1)}) %all-gather.5.cloned.1.call-update) | async-done | bytes 14155792 | tf_op jit(solution)/shard_map/all_gather | solution.py:256
  253.4 10.2 %fusion.10 = f32[1024,2304]{1,0:T(8,128)} fusion(bf16[1024,1024]{0,1:T(8,128)(2,1)} %multiply_convert_fusion.1, bf16[1024,6912]{1,0:T(8,128)(2,1)} %all-gather.5.cloned.1.call-done), kind=kOutput, calls=%fused_computation.28 | convolution fusion | flops 4831838208 | bytes 16252928 | tf_op jit(solution)/shard_map/dot_general | solution.py:30
  263.6 9.9 %fusion.21 = f32[2304,1024]{0,1:T(8,128)} fusion(bf16[1024,1024]{1,0:T(8,128)(2,1)S(1)} %copy-done.9, bf16[1024,6912]{1,0:T(8,128)(2,1)} %all-gather.5.cloned.1.call-done), kind=kOutput, calls=%fused_computation.44 | convolution fusion | flops 4831838208 | bytes 16252928 | tf_op jit(solution)/shard_map/dot_general | solution.py:30
  273.5 17.6 %fusion.2 = (bf16[1024,2304]{1,0:T(8,128)(2,1)}, bf16[1024,2304]{1,0:T(8,128)(2,1)}, bf16[1024,2304]{1,0:T(8,128)(2,1)}) fusion(f32[1024,2304]{1,0:T(8,128)} %fusion.10, f32[2304,1024]{0,1:T(8,128)} %fusion.21, bf16[1024,1024]{0,1:T(8,128)(2,1)S(1)} %copy-done.10, bf16[1024,6912]{1,0:T(8,128)(2,1)} %all-gather.5.cloned.1.call-done), kind=kOutput, calls=%fused_computation.5 | convolution fusion | flops 4869586944 | bytes 39845888 | tf_op jit(solution)/shard_map/dot_general | solution.py:30
  291.1 16.8 %fusion.3 = f32[1024,1024]{0,1:T(8,128)} fusion(bf16[1024,6912]{1,0:T(8,128)(2,1)} %all-gather.5.cloned.1.call-done, bf16[1024,2304]{1,0:T(8,128)(2,1)} %get-tuple-element.117, bf16[1024,2304]{1,0:T(8,128)(2,1)} %get-tuple-element.116), kind=kOutput, calls=%fused_computation.6 | convolution fusion | flops 9682550784 | bytes 23068672 | tf_op jit(solution)/shard_map/dot_general | solution.py:34
  307.9 9.1 %fusion.9 = bf16[1024,2304]{1,0:T(8,128)(2,1)} fusion(bf16[1024,2304]{1,0:T(8,128)(2,1)} %get-tuple-element.118, bf16[1024,1024]{1,0:T(8,128)(2,1)S(1)} %copy-done.9), kind=kOutput, calls=%fused_computation.27 | convolution fusion | flops 4834197504 | bytes 11534336 | tf_op jit(solution)/shard_map/dot_general | solution.py:40
  317.0 14.2 %convolution_convert_fusion = bf16[1024,4608]{1,0:T(8,128)(2,1)S(1)} fusion(bf16[1024,1024]{0,1:T(8,128)(2,1)} %multiply_convert_fusion.1, bf16[1024,2304]{1,0:T(8,128)(2,1)} %get-tuple-element.117, bf16[1024,2304]{1,0:T(8,128)(2,1)} %get-tuple-element.116), kind=kOutput, calls=%fused_computation.2 | convolution fusion | flops 9687269376 | bytes 20971520 | tf_op jit(solution)/shard_map/dot_general | solution.py:40
  331.2 9.1 %pad_maximum_fusion = bf16[1024,6912]{1,0:T(8,128)(2,1)} fusion(bf16[1024,2304]{1,0:T(8,128)(2,1)} %fusion.9, bf16[1024,4608]{1,0:T(8,128)(2,1)S(1)} %convolution_convert_fusion), kind=kLoop, calls=%fused_computation | loop fusion | flops 28311552 | bytes 28311552 | tf_op jit(solution)/shard_map/concatenate | solution.py:297
  340.4 6.8 add.72
  347.2 9.3 %fusion.25 = bf16[1024,1024]{0,1:T(8,128)(2,1)} fusion(bf16[1024,2304]{1,0:T(8,128)(2,1)} %get-tuple-element.118, bf16[1024,6912]{1,0:T(8,128)(2,1)} %all-gather.5.cloned.1.call-done), kind=kOutput, calls=%fused_computation.49 | convolution fusion | flops 4832886784 | bytes 11534336 | tf_op jit(solution)/shard_map/dot_general | solution.py:34
  357.1 2.9 copy.98
  360.0 4.7 multiply_reduce_fusion
  364.7 1.3 copy-done.4
  366.0 5.3 fusion.16
  371.2 4.4 convolution_convert_fusion.5.da_ref
  375.6 50.7 %attention_backward.1 = (bf16[1024,512]{1,0:T(8,128)(2,1)}, bf16[1024,256]{1,0:T(8,128)(2,1)}, bf16[1024,256]{1,0:T(8,128)(2,1)}, f32[2,1,64]{2,1,0:T(1,128)}, f32[2,1,64]{2,1,0:T(1,128)}) custom-call(f32[1024,1024]{1,0:T(8,128)} %fusion.29.q_ref.k_ref.v_ref, f32[1024,1024]{1,0:T(8,128)} %fusion.29.q_ref.k_ref.v_ref, ...), custom_call_target="tpu_custom_call" | custom-call | flops 20000000000 | bytes 10000000 | tf_op jit(solution)/shard_map/attention_backward/pallas_call | solution.py:195
  426.3 1.5 constant_dynamic-update-slice_fusion.6
  427.8 1.2 constant_dynamic-update-slice_fusion.5
  429.1 1.2 constant_dynamic-update-slice_fusion.4
  430.4 1.3 convolution_convert_fusion.4
  431.7 2.6 convolution_convert_fusion.2
  434.4 1.9 pad_maximum_fusion.4
  436.3 130.6 %reduce-scatter.5.cloned.1.call-done = bf16[64,6912]{1,0:T(8,128)(2,1)} async-done(((bf16[1024,6912]{1,0:T(8,128)(2,1)}), bf16[64,6912]{1,0:T(8,128)(2,1)}) %reduce-scatter.5.cloned.1.call-update) | async-done | bytes 884752 | tf_op jit(solution)/shard_map/reduce_scatter | solution.py:299
  567.0 4.6 copy.116
  571.7 5.9 convolution_convert_fusion.3
  577.6 4.0 copy.105
  582.1 4.3 fusion.15
  586.4 5.0 fusion.18
  591.4 4.0 copy.106
  595.5 40.5 %psum.7 = f32[2176]{0:T(1024)S(1)} all-reduce(f32[2176]{0:T(1024)S(1)} %concatenate.35), channel_id=1, replica_groups=mesh['fsdp'=16,'tensor'=2] {'fsdp','tensor'}, use_global_device_ids=true, to_apply=%region_12.13 | all-reduce | flops 2176 | bytes 17408 | tf_op jit(solution)/shard_map/psum | solution.py:330
  636.7 0.9 slice_bitcast_fusion
  637.6 1.1 fusion.43
  638.7 64.4 %reduce-scatter.7.cloned.1.call-done = bf16[64,1536]{1,0:T(8,128)(2,1)} async-done(((bf16[1024,1536]{1,0:T(8,128)(2,1)}), bf16[64,1536]{1,0:T(8,128)(2,1)}) %reduce-scatter.7.cloned.1.call-update) | async-done | bytes 196624
  703.1 1.1 copy.117
  (97 shorter events, 11.4 us)
Async XLA Ops:
  7.2 80.9 %copy-start.23 = (s32[1,8]{1,0:T(1,128)S(1)}, s32[1,8]{1,0:T(1,128)}, u32[]{:S(2)}) copy-start(s32[1,8]{1,0:T(1,128)} %param.15) | copy-start | bytes 100
  7.2 78.0 %all-gather.3.cloned.1.call-start = ((), (), s32[]{:S(2)}) async-start(), calls=%async_computation.2 | async-start | bytes 3620864 | tf_op jit(solution)/shard_map/all_gather | solution.py:254
  11.3 0.7 copy-start.14
  12.0 241.4 %all-gather.5.cloned.1.call-start = ((), (), s32[]{:S(2)}) async-start(), calls=%async_computation.3 | async-start | bytes 15040512 | tf_op jit(solution)/shard_map/all_gather | solution.py:256
  85.2 7.7 %copy-start.24 = (bf16[64]{0:T(256)(128)(2,1)S(1)}, bf16[64]{0:T(256)(128)(2,1)}, u32[]{:S(2)}) copy-start(bf16[64]{0:T(256)(128)(2,1)} %param.26) | copy-start | bytes 388
  85.2 7.7 %copy-start.25 = (bf16[64]{0:T(256)(128)(2,1)S(1)}, bf16[64]{0:T(256)(128)(2,1)}, u32[]{:S(2)}) copy-start(bf16[64]{0:T(256)(128)(2,1)} %param.25) | copy-start | bytes 388
  85.2 481.8 %reduce-scatter.5.cloned.1.call-start = ((), (), s32[]{:S(2)}) async-start(), calls=%async_computation.4 | async-start | bytes 15040512 | tf_op jit(solution)/shard_map/reduce_scatter | solution.py:299
  88.1 57.9 %copy-start.2 = (bf16[1024,1024]{0,1:T(8,128)(2,1)}, bf16[1024,1024]{0,1:T(8,128)(2,1)S(1)}, u32[]{:S(2)}) copy-start(bf16[1024,1024]{0,1:T(8,128)(2,1)S(1)} %copy.93) | copy-start | bytes 6291460
  89.6 4.8 copy-start.12
  93.8 0.6 copy-start.19
  94.4 4.8 copy-start.17
  94.7 4.5 copy-start.15
  138.7 7.2 %collective-permute-start = (f32[1024,1024]{0,1:T(8,128)S(1)}, f32[1024,1024]{0,1:T(8,128)S(1)}, u32[]{:S(2)}, u32[]{:S(2)}) collective-permute-start(f32[1024,1024]{0,1:T(8,128)S(1)} %fusion.34), channel_id=1, source_target_pairs={{0,1},{1,0},{2,3},{3,2},{4,5},{5,4},{6,7},{7,6},{8,9},{9,8},{10,11... | collective-permute-start | bytes 12582920 | tf_op jit(solution)/shard_map/ppermute | solution.py:223
  147.6 2.1 copy-start
  151.5 112.1 %copy-start.9 = (bf16[1024,1024]{1,0:T(8,128)(2,1)S(1)}, bf16[1024,1024]{1,0:T(8,128)(2,1)}, u32[]{:S(2)}) copy-start(bf16[1024,1024]{1,0:T(8,128)(2,1)} %param.27) | copy-start | bytes 6291460
  263.6 9.9 %copy-start.10 = (bf16[1024,1024]{0,1:T(8,128)(2,1)S(1)}, bf16[1024,1024]{0,1:T(8,128)(2,1)}, u32[]{:S(2)}) copy-start(bf16[1024,1024]{0,1:T(8,128)(2,1)} %multiply_convert_fusion.1) | copy-start | bytes 6291460
  307.9 32.5 %collective-permute-start.2 = (f32[1024,1024]{0,1:T(8,128)}, f32[1024,1024]{0,1:T(8,128)}, u32[]{:S(2)}, u32[]{:S(2)}) collective-permute-start(f32[1024,1024]{0,1:T(8,128)} %fusion.3), channel_id=1, source_target_pairs={{0,1},{1,0},{2,3},{3,2},{4,5},{5,4},{6,7},{7,6},{8,9},{9,8},{10,11... | collective-permute-start | bytes 12582920 | tf_op jit(solution)/shard_map/ppermute | solution.py:223
  347.2 355.9 %reduce-scatter.7.cloned.1.call-start = ((), (), s32[]{:S(2)}) async-start(), calls=%async_computation.5 | async-start | bytes 3342336
  356.6 8.1 %collective-permute-start.1 = (bf16[1024,1024]{0,1:T(8,128)(2,1)}, bf16[1024,1024]{0,1:T(8,128)(2,1)}, u32[]{:S(2)}, u32[]{:S(2)}) collective-permute-start(bf16[1024,1024]{0,1:T(8,128)(2,1)} %fusion.25), channel_id=1, source_target_pairs={{0,1},{1,0},{2,3},{3,2},{4,5},{5,4},{6,7},{7,6},{8,9},{9,8},{10,11... | collective-permute-start | bytes 6291464 | tf_op jit(solution)/shard_map/ppermute | solution.py:223
  359.9 4.8 copy-start.1
  359.9 6.0 copy-start.4
  371.2 4.4 copy-start.5
  375.6 54.7 %copy-start.11 = (bf16[1024,512]{1,0:T(8,128)(2,1)S(1)}, bf16[1024,512]{1,0:T(8,128)(2,1)}, u32[]{:S(2)}) copy-start(bf16[1024,512]{1,0:T(8,128)(2,1)} %get-tuple-element.29) | copy-start | bytes 3145732
  426.3 4.0 copy-start.6
  429.0 2.7 copy-start.3
  429.0 2.7 copy-start.16
  429.1 2.7 copy-start.18
  430.3 1.4 copy-start.13
  571.6 6.0 copy-start.22
  571.6 6.0 copy-start.21
  577.6 4.5 collective-permute-start.3
  581.6 4.8 copy-start.20
  581.6 4.8 copy-start.7
  591.4 45.2 %copy-start.8 = (bf16[64,6912]{1,0:T(8,128)(2,1)S(1)}, bf16[64,6912]{1,0:T(8,128)(2,1)}, u32[]{:S(2)}) copy-start(bf16[64,6912]{1,0:T(8,128)(2,1)} %reduce-scatter.5.cloned.1.call-done) | copy-start | bytes 2654212
Sparse Core Ops, SparseCore 0:
  12.1 73.0 all-gather.2
  87.9 165.3 all-gather.4
  347.3 219.5 reduce-scatter.4
  572.6 130.4 reduce-scatter.6
